TPU v7x, 32 devices: a whole 2x2x4 slice. The times are simulated.
32 devices in a mesh: rep: 4 (over x, core), fsdp: 8 (over z, y).
Axes of the slice: x: 2, y: 2, z: 4, core: 2. Of those that a mesh axis runs over, the one named last changes fastest.
Arguments:
- layer_in: bfloat16 [2, 8192, 1024], P(None, ('rep', 'fsdp')), may hold values from -6 to 6
- segments: int32 [2, 8192], P(None, ('rep', 'fsdp')), may hold values from 0 to 7, never falling along the last dimension, each value on 1 to 2000 neighbouring positions
- w_in: bfloat16 [1024, 3072], P(None, 'fsdp'), may hold values from -0.1875 to 0.1875
- w_out: bfloat16 [1024, 1024], P(None, 'fsdp'), may hold values from -0.1875 to 0.1875
- w_gate: bfloat16 [1024, 4608], P(None, 'fsdp'), may hold values from -0.1875 to 0.1875
- w_up: bfloat16 [1024, 4608], P(None, 'fsdp'), may hold values from -0.1875 to 0.1875
- w_down: bfloat16 [4608, 1024], P(None, 'fsdp'), may hold values from -0.09375 to 0.09375
- conv_taps: bfloat16 [3, 1024], P(None, 'fsdp'), may hold values from -3 to 3
- gain_one: bfloat16 [1024], P('fsdp'), may hold values from 0.099609375 to 1.8984375
- gain_two: bfloat16 [1024], P('fsdp'), may hold values from 0.099609375 to 1.8984375
- cotangent: bfloat16 [2, 8192, 1024], P(None, ('rep', 'fsdp')), may hold values from -6 to 6
Outputs:
- layer_out: float32 [2, 8192, 1024], P(None, ('rep', 'fsdp'))
- grad_layer_in: float32 [2, 8192, 1024], P(None, ('rep', 'fsdp'))
- grad_w_in: float32 [1024, 3072], P(None, 'fsdp')
- grad_w_out: float32 [1024, 1024], P(None, 'fsdp')
- grad_w_gate: float32 [1024, 4608], P(None, 'fsdp')
- grad_w_up: float32 [1024, 4608], P(None, 'fsdp')
- grad_w_down: float32 [4608, 1024], P(None, 'fsdp')
- grad_conv_taps: float32 [3, 1024], P(None, 'fsdp')
- grad_gain_one: float32 [1024], P('fsdp')
- grad_gain_two: float32 [1024], P('fsdp')
Inputs may be any that keep to these rules, and one draw needn't show every extreme that they name: `segments`: document numbers never fall along a micro-batch's 8192 tokens; a document holds at most 2000 tokens.
All inputs are finite; a program needn't handle non-finite values.
Results may differ from a plain program's by a relative error of at most 0.013.
Values may be sent and summed in bfloat16 or wider, within the bound.
A program may use at most 256 MiB of HBM per device.

v0:
```python
import jax
import jax.numpy as jnp
from jax import lax
from jax.sharding import PartitionSpec as P

epsilon = 1e-05


def shifted(block, axis, distance):
    devices = range(lax.axis_size(axis))
    route = [(i - distance, i) for i in devices if i - distance in devices]
    return lax.ppermute(block, axis, route)


def rms_scale(values):
    return lax.rsqrt(jnp.mean(values * values, axis=-1, keepdims=True) + epsilon)


def matmul(left_side, right_side):
    return jnp.dot(left_side, right_side, preferred_element_type=jnp.float32)


def contract_rows(left_side, right_side):
    return lax.dot_general(
        left_side, right_side, (((0,), (0,)), ((), ())), preferred_element_type=jnp.float32
    )


def against_rows(left_side, right_side):
    return lax.dot_general(
        left_side, right_side, (((1,), (1,)), ((), ())), preferred_element_type=jnp.float32
    )


def forward_pass(layer_rows, doc_rows, weights):
    w_in, w_out, w_gate, w_up, w_down, conv_taps, gain_one, gain_two = weights
    residual = layer_rows.astype(jnp.float32)
    model_width = residual.shape[1]
    seq_rows = residual.shape[0]
    tap_values = conv_taps.astype(jnp.float32)
    scale_one = rms_scale(residual)
    normed_one = (residual * scale_one * gain_one.astype(jnp.float32)).astype(jnp.bfloat16)
    projected = matmul(normed_one, w_in)
    b_part = projected[:, :model_width]
    c_part = projected[:, model_width : 2 * model_width]
    x_part = projected[:, 2 * model_width :]
    product_bx = b_part * x_part
    doc_float = doc_rows.astype(jnp.float32)
    rim_values, rim_ids = shifted((product_bx[-2:], doc_float[-2:]), "fsdp", 1)
    extended = jnp.concatenate([rim_values, product_bx], 0)
    extended_ids = jnp.concatenate([rim_ids, doc_float], 0)
    conv_out = tap_values[0] * product_bx
    doc_masks = []
    for offset in (1, 2):
        matching = (extended_ids[2 - offset : 2 - offset + seq_rows] == doc_float).astype(
            jnp.float32
        )[:, None]
        doc_masks.append(matching)
        conv_out = (
            conv_out + tap_values[offset] * matching * extended[2 - offset : 2 - offset + seq_rows]
        )
    gated_rows = (c_part * conv_out).astype(jnp.bfloat16)
    middle = residual + matmul(gated_rows, w_out)
    scale_two = rms_scale(middle)
    normed_two = (middle * scale_two * gain_two.astype(jnp.float32)).astype(jnp.bfloat16)
    gate_pre = matmul(normed_two, w_gate)
    up_pre = matmul(normed_two, w_up)
    hidden = (jax.nn.silu(gate_pre) * up_pre).astype(jnp.bfloat16)
    output = middle + matmul(hidden, w_down)
    saved_state = (
        residual,
        scale_one,
        normed_one,
        projected,
        extended,
        doc_masks,
        conv_out,
        gated_rows,
        middle,
        scale_two,
        normed_two,
        gate_pre,
        up_pre,
        hidden,
    )
    return (output, saved_state)


def backward_pass(cotan_rows, weights, saved_state):
    w_in, w_out, w_gate, w_up, w_down, conv_taps, gain_one, gain_two = weights
    (
        residual,
        scale_one,
        normed_one,
        projected,
        extended,
        doc_masks,
        conv_out,
        gated_rows,
        middle,
        scale_two,
        normed_two,
        gate_pre,
        up_pre,
        hidden,
    ) = saved_state
    model_width = residual.shape[1]
    seq_rows = residual.shape[0]
    tap_values = conv_taps.astype(jnp.float32)
    b_part = projected[:, :model_width]
    c_part = projected[:, model_width : 2 * model_width]
    x_part = projected[:, 2 * model_width :]
    grad_out = cotan_rows.astype(jnp.float32)
    grad_down = contract_rows(hidden, cotan_rows)
    grad_hidden = against_rows(cotan_rows, w_down)
    gate_prob = jax.nn.sigmoid(gate_pre)
    grad_gate = (grad_hidden * up_pre * gate_prob * (1.0 + gate_pre * (1.0 - gate_prob))).astype(
        jnp.bfloat16
    )
    grad_up = (grad_hidden * gate_pre * gate_prob).astype(jnp.bfloat16)
    grad_wgate = contract_rows(normed_two, grad_gate)
    grad_wup = contract_rows(normed_two, grad_up)
    grad_normed_two = against_rows(grad_gate, w_gate) + against_rows(grad_up, w_up)
    grad_gtwo = jnp.sum(grad_normed_two * middle * scale_two, axis=0)
    weighted = grad_normed_two * gain_two.astype(jnp.float32)
    grad_middle = (
        grad_out
        + scale_two * weighted
        - middle * scale_two**3 * jnp.mean(weighted * middle, axis=-1, keepdims=True)
    )
    grad_branch = grad_middle.astype(jnp.bfloat16)
    grad_wout = contract_rows(gated_rows, grad_branch)
    grad_gated = against_rows(grad_branch, w_out)
    grad_c = grad_gated * conv_out
    grad_conv = grad_gated * c_part
    grad_ext = jnp.pad(tap_values[0] * grad_conv, ((2, 0), (0, 0)))
    tap_rows = [jnp.sum(grad_conv * extended[2:], axis=0)]
    for offset, matching in zip((1, 2), doc_masks):
        masked_grad = matching * grad_conv
        grad_ext = grad_ext + jnp.pad(
            tap_values[offset] * masked_grad, ((2 - offset, offset), (0, 0))
        )
        tap_rows.append(jnp.sum(masked_grad * extended[2 - offset : 2 - offset + seq_rows], axis=0))
    rim_back = shifted(grad_ext[:2], "fsdp", -1)
    grad_bx = grad_ext[2:] + jnp.pad(rim_back, ((seq_rows - 2, 0), (0, 0)))
    grad_taps = jnp.stack(tap_rows)
    grad_proj = jnp.concatenate([grad_bx * x_part, grad_c, grad_bx * b_part], 1).astype(
        jnp.bfloat16
    )
    grad_win = contract_rows(normed_one, grad_proj)
    grad_normed_one = against_rows(grad_proj, w_in)
    grad_gone = jnp.sum(grad_normed_one * residual * scale_one, axis=0)
    weighted_one = grad_normed_one * gain_one.astype(jnp.float32)
    grad_input = (
        grad_middle
        + scale_one * weighted_one
        - residual * scale_one**3 * jnp.mean(weighted_one * residual, axis=-1, keepdims=True)
    )
    local_grads = (
        grad_win,
        grad_wout,
        grad_wgate,
        grad_wup,
        grad_down,
        grad_taps,
        grad_gone,
        grad_gtwo,
    )
    return (grad_input, local_grads)


def per_device(
    layer_in, segments, w_in, w_out, w_gate, w_up, w_down, conv_taps, gain_one, gain_two, cotangent
):
    outputs = []
    input_grads = []
    totals = None
    owned_grads = None
    for batch_index in range(layer_in.shape[0]):
        weights_now = (
            lax.all_gather(w_in, "fsdp", axis=1, tiled=True),
            lax.all_gather(w_out, "fsdp", axis=1, tiled=True),
            lax.all_gather(w_gate, "fsdp", axis=1, tiled=True),
            lax.all_gather(w_up, "fsdp", axis=1, tiled=True),
            lax.all_gather(w_down, "fsdp", axis=1, tiled=True),
            lax.all_gather(conv_taps, "fsdp", axis=1, tiled=True),
            lax.all_gather(gain_one, "fsdp", axis=0, tiled=True),
            lax.all_gather(gain_two, "fsdp", axis=0, tiled=True),
        )
        output, saved_state = forward_pass(
            layer_in[batch_index], segments[batch_index], weights_now
        )
        outputs.append(output)
        grad_input, local_grads = backward_pass(cotangent[batch_index], weights_now, saved_state)
        input_grads.append(grad_input)
        totals = local_grads if batch_index == 0 else jax.tree.map(jnp.add, totals, local_grads)
    owned_grads = (
        lax.psum_scatter(totals[0], "fsdp", scatter_dimension=1, tiled=True),
        lax.psum_scatter(totals[1], "fsdp", scatter_dimension=1, tiled=True),
        lax.psum_scatter(totals[2], "fsdp", scatter_dimension=1, tiled=True),
        lax.psum_scatter(totals[3], "fsdp", scatter_dimension=1, tiled=True),
        lax.psum_scatter(totals[4], "fsdp", scatter_dimension=1, tiled=True),
        lax.psum_scatter(totals[5], "fsdp", scatter_dimension=1, tiled=True),
        lax.psum_scatter(totals[6], "fsdp", scatter_dimension=0, tiled=True),
        lax.psum_scatter(totals[7], "fsdp", scatter_dimension=0, tiled=True),
    )
    summed = (
        lax.psum(owned_grads[0].astype(jnp.bfloat16), "rep").astype(jnp.float32),
        lax.psum(owned_grads[1].astype(jnp.bfloat16), "rep").astype(jnp.float32),
        lax.psum(owned_grads[2].astype(jnp.bfloat16), "rep").astype(jnp.float32),
        lax.psum(owned_grads[3].astype(jnp.bfloat16), "rep").astype(jnp.float32),
        lax.psum(owned_grads[4].astype(jnp.bfloat16), "rep").astype(jnp.float32),
        lax.psum(owned_grads[5].astype(jnp.bfloat16), "rep").astype(jnp.float32),
        lax.psum(owned_grads[6].astype(jnp.bfloat16), "rep").astype(jnp.float32),
        lax.psum(owned_grads[7].astype(jnp.bfloat16), "rep").astype(jnp.float32),
    )
    return (
        jnp.stack(outputs),
        jnp.stack(input_grads),
        summed[0],
        summed[1],
        summed[2],
        summed[3],
        summed[4],
        summed[5],
        summed[6],
        summed[7],
    )


def solution(mesh):
    return jax.shard_map(
        per_device,
        mesh=mesh,
        in_specs=(
            P(None, ("rep", "fsdp"), None),
            P(None, ("rep", "fsdp")),
            P(None, "fsdp"),
            P(None, "fsdp"),
            P(None, "fsdp"),
            P(None, "fsdp"),
            P(None, "fsdp"),
            P(None, "fsdp"),
            P("fsdp"),
            P("fsdp"),
            P(None, ("rep", "fsdp"), None),
        ),
        out_specs=(
            P(None, ("rep", "fsdp"), None),
            P(None, ("rep", "fsdp"), None),
            P(None, "fsdp"),
            P(None, "fsdp"),
            P(None, "fsdp"),
            P(None, "fsdp"),
            P(None, "fsdp"),
            P(None, "fsdp"),
            P("fsdp"),
            P("fsdp"),
        ),
        check_vma=False,
    )
```

profile of v0, /device:TPU:0, one launch (start us, length us, event | category | flops | bytes accessed | tf_op | source)
XLA Modules:
  0.0 2077.8 jit_solution(5264892604067919988)
XLA Ops:
  19.1 18.1 all-gather
  37.2 16.5 all-gather.1
  53.7 18.4 all_gather.34
  73.8 39.2 %all-gather.8.cloned.1.call-done = bf16[1024,3072]{1,0:T(8,128)(2,1)} async-done(((bf16[1024,384]{1,0:T(8,128)(2,1)}), bf16[1024,3072]{1,0:T(8,128)(2,1)}) %all-gather.8.cloned.1.call-update) | async-done | bytes 6291472 | tf_op jit(solution)/shard_map/all_gather | solution.py:181
  128.9 35.5 %all-gather.10.cloned.1.call-done = bf16[1024,1024]{1,0:T(8,128)(2,1)} async-done(((bf16[1024,128]{1,0:T(8,128)(2,1)}), bf16[1024,1024]{1,0:T(8,128)(2,1)}) %all-gather.10.cloned.1.call-update) | async-done | bytes 2097168 | tf_op jit(solution)/shard_map/all_gather | solution.py:182
  169.1 133.8 %all-gather.12.cloned.1.call-done = bf16[1024,4608]{0,1:T(8,128)(2,1)} async-done(((bf16[1024,576]{0,1:T(8,128)(2,1)}), bf16[1024,4608]{0,1:T(8,128)(2,1)}) %all-gather.12.cloned.1.call-update) | async-done | bytes 9437200 | tf_op jit(solution)/shard_map/all_gather | solution.py:183
  302.9 11.5 fusion.54
  314.4 126.8 %all-gather.14.cloned.1.call-done = bf16[1024,4608]{0,1:T(8,128)(2,1)} async-done(((bf16[1024,576]{0,1:T(8,128)(2,1)}), bf16[1024,4608]{0,1:T(8,128)(2,1)}) %all-gather.14.cloned.1.call-update) | async-done | bytes 9437200 | tf_op jit(solution)/shard_map/all_gather | solution.py:184
  441.2 11.5 fusion.55
  452.7 126.8 %all-gather.16.cloned.1.call-done = bf16[4608,1024]{1,0:T(8,128)(2,1)} async-done(((bf16[4608,128]{1,0:T(8,128)(2,1)}), bf16[4608,1024]{1,0:T(8,128)(2,1)}) %all-gather.16.cloned.1.call-update) | async-done | bytes 9437200 | tf_op jit(solution)/shard_map/all_gather | solution.py:185
  579.5 13.6 multiply_convert_fusion.2
  593.2 6.9 fusion.58
  600.1 6.0 multiply_reduce_fusion.1
  611.6 11.5 fusion.56
  623.2 13.1 multiply_convert_fusion
  636.3 6.9 fusion.59
  672.5 6.5 convolution_add_fusion.3
  679.2 11.2 fusion.61
  690.5 12.7 convolution_add_fusion.1
  703.2 11.2 fusion.60
  714.4 12.8 convolution_add_fusion.2
  727.3 11.0 fusion.28
  738.3 12.1 convolution_add_fusion
  753.7 7.3 fusion
  769.5 181.9 %reduce-scatter.9.cloned.1.call-done = f32[1024,384]{1,0:T(8,128)} async-done(((f32[1024,3072]{1,0:T(8,128)}), f32[1024,384]{1,0:T(8,128)}) %reduce-scatter.9.cloned.1.call-update) | async-done | bytes 1572880 | tf_op jit(solution)/shard_map/reduce_scatter | solution.py:198
  953.7 314.4 %reduce-scatter.15.cloned.1.call-done = f32[1024,576]{0,1:T(8,128)} async-done(((f32[1024,4608]{0,1:T(8,128)}), f32[1024,576]{0,1:T(8,128)}) %reduce-scatter.15.cloned.1.call-update) | async-done | bytes 2359312 | tf_op jit(solution)/shard_map/reduce_scatter | solution.py:201
  1271.0 314.0 %reduce-scatter.13.cloned.1.call-done = f32[1024,576]{0,1:T(8,128)} async-done(((f32[1024,4608]{0,1:T(8,128)}), f32[1024,576]{0,1:T(8,128)}) %reduce-scatter.13.cloned.1.call-update) | async-done | bytes 2359312 | tf_op jit(solution)/shard_map/reduce_scatter | solution.py:200
  1587.8 314.8 %reduce-scatter.17.cloned.1.call-done = f32[4608,128]{1,0:T(8,128)} async-done(((f32[4608,1024]{1,0:T(8,128)}), f32[4608,128]{1,0:T(8,128)}) %reduce-scatter.17.cloned.1.call-update) | async-done | bytes 2359312 | tf_op jit(solution)/shard_map/reduce_scatter | solution.py:202
  1910.7 6.4 fusion.12
  1917.1 19.8 all-reduce.10
  1940.7 26.8 %reduce-scatter.19.cloned.1.call-done = f32[128,3]{1,0:T(8,128)} async-done(((f32[1024,3]{1,0:T(8,128)}), f32[128,3]{1,0:T(8,128)}) %reduce-scatter.19.cloned.1.call-update) | async-done | bytes 1552
  1975.7 86.6 %all-reduce.15.cloned.1.call-done = (bf16[1024,384]{1,0:T(8,128)(2,1)}, bf16[1024,128]{1,0:T(8,128)(2,1)}, bf16[1024,576]{0,1:T(8,128)(2,1)}, bf16[1024,576]{0,1:T(8,128)(2,1)}, bf16[4608,128]{1,0:T(8,128)(2,1)}) async-done(((bf16[1024,384]{1,0:T(8,128)(2,1)}, bf16[1024,128]{1,0:T(8,128)(2,1)}, bf16[1024,576]{0,1:T(8,128)(2,1)}, bf16[1024,576]{0,1:T(8,128)(2,1)}, bf16[4608,128]{1,0:T(8,128)(2,1)}), ...) | async-done | bytes 4587536 | tf_op jit(solution)/shard_map/psum | solution.py:208
  (225 shorter events, 116.3 us)
Async XLA Ops:
  7.2 11.9 copy-start.54
  7.2 30.0 %copy-start.55 = (bf16[128]{0:T(256)(128)(2,1)S(1)}, bf16[128]{0:T(256)(128)(2,1)}, u32[]{:S(2)}) copy-start(bf16[128]{0:T(256)(128)(2,1)} %param.20) | copy-start | bytes 772
  7.2 46.5 %copy-start.53 = (bf16[3,128]{1,0:T(4,128)(2,1)S(1)}, bf16[3,128]{1,0:T(4,128)(2,1)}, u32[]{:S(2)}) copy-start(bf16[3,128]{1,0:T(4,128)(2,1)} %param.18) | copy-start | bytes 2308
  7.2 64.9 %copy-start.4 = (bf16[2,256,1024]{2,1,0:T(8,128)(2,1)S(1)}, bf16[2,256,1024]{2,1,0:T(8,128)(2,1)}, u32[]{:S(2)}) copy-start(bf16[2,256,1024]{2,1,0:T(8,128)(2,1)} %param.11) | copy-start | bytes 3145732
  7.2 105.7 %all-gather.8.cloned.1.call-start = ((), (), s32[]{:S(2)}) async-start(), calls=%async_computation.6 | async-start | bytes 7077888 | tf_op jit(solution)/shard_map/all_gather | solution.py:181
  8.0 156.5 %all-gather.10.cloned.1.call-start = ((), (), s32[]{:S(2)}) async-start(), calls=%async_computation.7 | async-start | bytes 2359296 | tf_op jit(solution)/shard_map/all_gather | solution.py:182
  8.7 294.2 %all-gather.12.cloned.1.call-start = ((), (), s32[]{:S(2)}) async-start(), calls=%async_computation.8 | async-start | bytes 10616832 | tf_op jit(solution)/shard_map/all_gather | solution.py:183
  9.4 431.8 %all-gather.14.cloned.1.call-start = ((), (), s32[]{:S(2)}) async-start(), calls=%async_computation.9 | async-start | bytes 10616832 | tf_op jit(solution)/shard_map/all_gather | solution.py:184
  10.0 569.5 %all-gather.16.cloned.1.call-start = ((), (), s32[]{:S(2)}) async-start(), calls=%async_computation.10 | async-start | bytes 10616832 | tf_op jit(solution)/shard_map/all_gather | solution.py:185
  10.6 757.1 %reduce-scatter.11.cloned.1.call-start = ((), (), s32[]{:S(2)}) async-start(), calls=%async_computation.12 | async-start | bytes 4718592 | tf_op jit(solution)/shard_map/reduce_scatter | solution.py:199
  10.8 62.8 %collective-permute-start = (f32[2]{0:T(128)S(1)}, f32[2]{0:T(128)S(1)}, u32[]{:S(2)}, u32[]{:S(2)}) collective-permute-start(f32[2]{0:T(128)S(1)} %slice_bitcast_fusion.1), channel_id=1, source_target_pairs={{0,1},{1,2},{2,3},{3,4},{4,5},{5,6},{6,7},{8,9},{9,10},{10,11},{11... | collective-permute-start | bytes 32 | tf_op jit(solution)/shard_map/ppermute | solution.py:12
  15.7 58.0 %collective-permute-start.2 = (f32[2]{0:T(128)S(1)}, f32[2]{0:T(128)S(1)}, u32[]{:S(2)}, u32[]{:S(2)}) collective-permute-start(f32[2]{0:T(128)S(1)} %slice_bitcast_fusion), channel_id=1, source_target_pairs={{0,1},{1,2},{2,3},{3,4},{4,5},{5,6},{6,7},{8,9},{9,10},{10,11},{11... | collective-permute-start | bytes 32 | tf_op jit(solution)/shard_map/ppermute | solution.py:12
  117.9 7.6 collective-permute-start.1
  123.3 3.3 collective-permute-start.3
  169.1 272.2 %copy-start.12 = (bf16[256,1024]{1,0:T(8,128)(2,1)}, bf16[256,1024]{1,0:T(8,128)(2,1)S(1)}, u32[]{:S(2)}) copy-start(bf16[256,1024]{1,0:T(8,128)(2,1)S(1)} %multiply_convert_fusion.14) | copy-start | bytes 1572868
  314.4 265.1 %copy-start.13 = (bf16[2,256,1024]{2,1,0:T(8,128)(2,1)S(1)}, bf16[2,256,1024]{2,1,0:T(8,128)(2,1)}, u32[]{:S(2)}) copy-start(bf16[2,256,1024]{2,1,0:T(8,128)(2,1)} %param.21) | copy-start | bytes 3145732
  653.5 297.9 %reduce-scatter.9.cloned.1.call-start = ((), (), s32[]{:S(2)}) async-start(), calls=%async_computation.11 | async-start | bytes 14155776 | tf_op jit(solution)/shard_map/reduce_scatter | solution.py:198
  659.1 11.4 copy-start.36
  661.4 11.1 copy-start.31
  661.9 5.5 collective-permute-start.4
  663.9 6.2 collective-permute-start.5
  679.0 589.1 %reduce-scatter.15.cloned.1.call-start = ((), (), s32[]{:S(2)}) async-start(), calls=%async_computation.14 | async-start | bytes 21233664 | tf_op jit(solution)/shard_map/reduce_scatter | solution.py:201
  679.2 11.2 copy-start.24
  679.2 11.2 copy-start.29
  703.2 881.8 %reduce-scatter.13.cloned.1.call-start = ((), (), s32[]{:S(2)}) async-start(), calls=%async_computation.13 | async-start | bytes 21233664 | tf_op jit(solution)/shard_map/reduce_scatter | solution.py:200
  703.2 11.2 copy-start.22
  703.2 11.2 copy-start.30
  727.2 1175.3 %reduce-scatter.17.cloned.1.call-start = ((), (), s32[]{:S(2)}) async-start(), calls=%async_computation.15 | async-start | bytes 21233664 | tf_op jit(solution)/shard_map/reduce_scatter | solution.py:202
  750.4 1217.1 %reduce-scatter.19.cloned.1.call-start = ((), (), s32[]{:S(2)}) async-start(), calls=%async_computation.16 | async-start | bytes 589824
  753.4 1308.9 %all-reduce.15.cloned.1.call-start = ((), (), s32[]{:S(2)}) async-start(), calls=%async_computation.17 | async-start | bytes 9175040 | tf_op jit(solution)/shard_map/psum | solution.py:208
  1910.7 26.4 %copy-start.49 = (f32[256]{0:T(256)S(1)}, f32[256]{0:T(256)}, u32[]{:S(2)}) copy-start(f32[256]{0:T(256)} %get-tuple-element.81) | copy-start | bytes 3076
  1910.7 26.4 %copy-start.50 = (f32[256]{0:T(256)S(1)}, f32[256]{0:T(256)}, u32[]{:S(2)}) copy-start(f32[256]{0:T(256)} %get-tuple-element.83) | copy-start | bytes 3076
  (44 other events, 206.0 us)
Sparse Core Ops, SparseCore 0:
  10.1 102.7 all-gather.7
  115.0 49.4 all-gather.9
  166.6 136.2 all-gather.11
  304.9 136.2 all-gather.13
  443.1 136.3 all-gather.15
  653.6 86.6 reduce-scatter.10
  744.3 207.0 reduce-scatter.8
  955.7 312.3 reduce-scatter.14
  1272.5 312.3 reduce-scatter.12
  1589.2 313.3 reduce-scatter.16
  1906.3 61.1 reduce-scatter.18
  1970.6 91.6 all-reduce.14
where the time goes:
time: 2080 us
  waiting for transfers between devices  1710 us (82%)
  matrix products  213 us (10%)
  blocking collectives  78.4 us (4%)
  other arithmetic  36.1 us (2%)
    reduce_scatter x1, waiting for transfers between devices, per_device(): lax.psum_scatter(totals[4], 'fsdp', scatter_dimension=1, tiled=True)  315 us
    reduce_scatter x1, waiting for transfers between devices, per_device(): lax.psum_scatter(totals[3], 'fsdp', scatter_dimension=1, tiled=True)  314 us
    reduce_scatter x1, waiting for transfers between devices, per_device(): lax.psum_scatter(totals[2], 'fsdp', scatter_dimension=1, tiled=True)  314 us
    reduce_scatter x1, waiting for transfers between devices, per_device(): lax.psum_scatter(totals[0], 'fsdp', scatter_dimension=1, tiled=True)  182 us
    all_gather x1, waiting for transfers between devices, per_device(): lax.all_gather(w_gate, 'fsdp', axis=1, tiled=True)  134 us
    all_gather x1, waiting for transfers between devices, per_device(): lax.all_gather(w_down, 'fsdp', axis=1, tiled=True)  127 us
    all_gather x1, waiting for transfers between devices, per_device(): lax.all_gather(w_up, 'fsdp', axis=1, tiled=True)  127 us
    psum x1, waiting for transfers between devices, per_device(): lax.psum(owned_grads[0].astype(jnp.bfloat16), 'rep').astype(jnp.float32)  86.6 us
  transfers between devices with their start and end apart: 18, of which 14 were waited for; matrix products, arithmetic and copies ran while one was open for 8% of the time, Pallas kernels for 0%

commit v1 on v0

--- a/solution.py
+++ b/solution.py
@@ -194,15 +194,11 @@
         grad_input, local_grads = backward_pass(cotangent[batch_index], weights_now, saved_state)
         input_grads.append(grad_input)
         totals = local_grads if batch_index == 0 else jax.tree.map(jnp.add, totals, local_grads)
-    owned_grads = (
-        lax.psum_scatter(totals[0], "fsdp", scatter_dimension=1, tiled=True),
-        lax.psum_scatter(totals[1], "fsdp", scatter_dimension=1, tiled=True),
-        lax.psum_scatter(totals[2], "fsdp", scatter_dimension=1, tiled=True),
-        lax.psum_scatter(totals[3], "fsdp", scatter_dimension=1, tiled=True),
-        lax.psum_scatter(totals[4], "fsdp", scatter_dimension=1, tiled=True),
-        lax.psum_scatter(totals[5], "fsdp", scatter_dimension=1, tiled=True),
-        lax.psum_scatter(totals[6], "fsdp", scatter_dimension=0, tiled=True),
-        lax.psum_scatter(totals[7], "fsdp", scatter_dimension=0, tiled=True),
+    owned_grads = tuple(
+        lax.psum_scatter(
+            total.astype(jnp.bfloat16), "fsdp", scatter_dimension=total.ndim - 1, tiled=True
+        )
+        for total in totals
     )
     summed = (
         lax.psum(owned_grads[0].astype(jnp.bfloat16), "rep").astype(jnp.float32),

time: 2080 us -> 1520 us (0.73)
  waiting for transfers between devices: 1710 us -> 1130 us
  local copies, waits for them, and re-layouts: 7.12 us -> 38.5 us
    reduce_scatter x5 -> x2, waiting for transfers between devices: 1120 us -> 330 us  [per_device(): lax.psum_scatter(total.astype(jnp.bfloat16), 'fsdp', scatter_dimension=to...]
    unnamed x13 -> x16, waiting for transfers between devices: 30 us -> 246 us
    unnamed x121 -> x119, local copies, waits for them, and re-layouts: 6.95 us -> 38.4 us
  transfers between devices with their start and end apart: 18 -> 18, of which waited for: 14 -> 14; matrix products, arithmetic and copies ran while one was open for 8% -> 12% of each run, Pallas kernels for 0% -> 0%
where the time goes in v1:
time: 1520 us
  waiting for transfers between devices  1130 us (74%)
  matrix products  212 us (14%)
  blocking collectives  78.1 us (5%)
  local copies, waits for them, and re-layouts  38.5 us (3%)
  other arithmetic  23.3 us (2%)
  starting transfers between devices  17.8 us (1%)
  between operations  16 us (1%)
    reduce_scatter x2, waiting for transfers between devices, per_device(): lax.psum_scatter(total.astype(jnp.bfloat16), 'fsdp', scatter_dimension=to...  330 us
    unnamed x16, waiting for transfers between devices  246 us
    all_gather x1, waiting for transfers between devices, per_device(): lax.all_gather(w_gate, 'fsdp', axis=1, tiled=True)  134 us
    all_gather x1, waiting for transfers between devices, per_device(): lax.all_gather(w_up, 'fsdp', axis=1, tiled=True)  127 us
    all_gather x1, waiting for transfers between devices, per_device(): lax.all_gather(w_down, 'fsdp', axis=1, tiled=True)  127 us
    psum x1, waiting for transfers between devices, per_device(): lax.psum(owned_grads[0].astype(jnp.bfloat16), 'rep').astype(jnp.float32)  86.7 us
    dot_general x10, matrix products, contract_rows(): lax.dot_general(left_side, right_side, (((0,), (0,)), ((), ())), preferre...  81.4 us
    dot_general x10, matrix products, against_rows(): lax.dot_general(left_side, right_side, (((1,), (1,)), ((), ())), preferre...  66.9 us
  transfers between devices with their start and end apart: 18, of which 14 were waited for; matrix products, arithmetic and copies ran while one was open for 12% of the time, Pallas kernels for 0%

profile of v1, /device:TPU:0, one launch (start us, length us, event | category | flops | bytes accessed | tf_op | source)
XLA Modules:
  0.0 1515.9 jit_solution(18098147917205312811)
XLA Ops:
  19.1 18.1 %all-gather = bf16[8,1,128]{2,1,0:T(2,128)(2,1)S(1)} all-gather(bf16[1,1,128]{2,1,0:T(2,128)(2,1)S(1)} %bitcast.150), channel_id=1, replica_groups=mesh['rep'=4,'fsdp'=8] {'fsdp'}, dimensions={0}, use_global_device_ids=true | all-gather | bytes 2304 | tf_op jit(solution)/shard_map/all_gather | solution.py:187
  37.2 16.5 %all-gather.1 = bf16[8,1,128]{2,1,0:T(2,128)(2,1)S(1)} all-gather(bf16[1,1,128]{2,1,0:T(2,128)(2,1)S(1)} %bitcast.151), channel_id=1, replica_groups=mesh['rep'=4,'fsdp'=8] {'fsdp'}, dimensions={0}, use_global_device_ids=true | all-gather | bytes 2304 | tf_op jit(solution)/shard_map/all_gather | solution.py:188
  53.7 18.4 %all_gather.34 = bf16[3,1024]{1,0:T(4,128)(2,1)S(1)} all-gather(bf16[3,128]{1,0:T(4,128)(2,1)S(1)} %copy-done.49), channel_id=1, replica_groups=mesh['rep'=4,'fsdp'=8] {'fsdp'}, dimensions={1}, use_global_device_ids=true | all-gather | bytes 6912 | tf_op jit(solution)/shard_map/all_gather | solution.py:186
  73.8 39.2 %all-gather.8.cloned.1.call-done = bf16[1024,3072]{1,0:T(8,128)(2,1)} async-done(((bf16[1024,384]{1,0:T(8,128)(2,1)}), bf16[1024,3072]{1,0:T(8,128)(2,1)}) %all-gather.8.cloned.1.call-update) | async-done | bytes 6291472 | tf_op jit(solution)/shard_map/all_gather | solution.py:181
  128.9 35.5 %all-gather.10.cloned.1.call-done = bf16[1024,1024]{1,0:T(8,128)(2,1)} async-done(((bf16[1024,128]{1,0:T(8,128)(2,1)}), bf16[1024,1024]{1,0:T(8,128)(2,1)}) %all-gather.10.cloned.1.call-update) | async-done | bytes 2097168 | tf_op jit(solution)/shard_map/all_gather | solution.py:182
  168.9 134.0 %all-gather.12.cloned.1.call-done = bf16[1024,4608]{0,1:T(8,128)(2,1)} async-done(((bf16[1024,576]{0,1:T(8,128)(2,1)}), bf16[1024,4608]{0,1:T(8,128)(2,1)}) %all-gather.12.cloned.1.call-update) | async-done | bytes 9437200 | tf_op jit(solution)/shard_map/all_gather | solution.py:183
  302.9 11.5 fusion.55
  314.4 126.9 %all-gather.14.cloned.1.call-done = bf16[1024,4608]{0,1:T(8,128)(2,1)} async-done(((bf16[1024,576]{0,1:T(8,128)(2,1)}), bf16[1024,4608]{0,1:T(8,128)(2,1)}) %all-gather.14.cloned.1.call-update) | async-done | bytes 9437200 | tf_op jit(solution)/shard_map/all_gather | solution.py:184
  441.2 11.5 fusion.56
  452.7 126.8 %all-gather.16.cloned.1.call-done = bf16[4608,1024]{1,0:T(8,128)(2,1)} async-done(((bf16[4608,128]{1,0:T(8,128)(2,1)}), bf16[4608,1024]{1,0:T(8,128)(2,1)}) %all-gather.16.cloned.1.call-update) | async-done | bytes 9437200 | tf_op jit(solution)/shard_map/all_gather | solution.py:185
  579.5 13.6 multiply_convert_fusion.2
  593.2 6.9 fusion.59
  611.6 11.5 fusion.57
  623.1 13.1 multiply_convert_fusion
  636.2 6.9 fusion.60
  679.9 8.7 copy.21
  688.8 10.9 fusion.28
  699.7 11.4 add_convert_fusion
  711.1 12.8 copy.25
  724.0 11.3 fusion.62
  735.3 13.6 add_convert_fusion.1
  749.2 11.3 fusion.61
  760.5 13.7 add_convert_fusion.2
  777.4 7.5 fusion
  793.5 49.8 %reduce-scatter.19.cloned.1.call-done = bf16[384,1024]{1,0:T(8,128)(2,1)} async-done(((bf16[3072,1024]{1,0:T(8,128)(2,1)}), bf16[384,1024]{1,0:T(8,128)(2,1)}) %reduce-scatter.19.cloned.1.call-update) | async-done | bytes 786448
  845.6 163.9 %reduce-scatter.23.cloned.1.call-done = bf16[128,4608]{1,0:T(8,128)(2,1)} async-done(((bf16[1024,4608]{1,0:T(8,128)(2,1)}), bf16[128,4608]{1,0:T(8,128)(2,1)}) %reduce-scatter.23.cloned.1.call-update) | async-done | bytes 1179664
  1011.9 163.8 %reduce-scatter.17.cloned.1.call-done = bf16[1024,576]{0,1:T(8,128)(2,1)} async-done(((bf16[1024,4608]{0,1:T(8,128)(2,1)}), bf16[1024,576]{0,1:T(8,128)(2,1)}) %reduce-scatter.17.cloned.1.call-update) | async-done | bytes 1179664 | tf_op jit(solution)/shard_map/reduce_scatter | solution.py:198
  1175.7 166.1 %reduce-scatter.15.cloned.1.call-done = bf16[1024,576]{0,1:T(8,128)(2,1)} async-done(((bf16[1024,4608]{0,1:T(8,128)(2,1)}), bf16[1024,576]{0,1:T(8,128)(2,1)}) %reduce-scatter.15.cloned.1.call-update) | async-done | bytes 1179664 | tf_op jit(solution)/shard_map/reduce_scatter | solution.py:198
  1347.1 6.4 fusion.12
  1353.5 19.5 %all-reduce.10 = (bf16[1024]{0:T(1024)(128)(2,1)S(1)}, bf16[1024]{0:T(1024)(128)(2,1)S(1)}) all-reduce(bf16[1024]{0:T(1024)(128)(2,1)S(1)} %add_convert_fusion.6, bf16[1024]{0:T(1024)(128)(2,1)S(1)} %add_convert_fusion.5), channel_id=8, replica_groups=mesh['rep'=4,'fsdp'=8] {'fsdp'}, use_global_device_ids=true, to_apply=%region_28.29.clone | all-reduce | flops 2048 | bytes 8192
  1376.8 28.7 %reduce-scatter.25.cloned.1.call-done = bf16[128,3]{1,0:T(8,128)(2,1)} async-done(((bf16[1024,3]{1,0:T(8,128)(2,1)}), bf16[128,3]{1,0:T(8,128)(2,1)}) %reduce-scatter.25.cloned.1.call-update) | async-done | bytes 784
  1413.6 86.7 %all-reduce.15.cloned.1.call-done = (bf16[1024,384]{1,0:T(8,128)(2,1)}, bf16[1024,128]{1,0:T(8,128)(2,1)}, bf16[1024,576]{0,1:T(8,128)(2,1)}, bf16[1024,576]{0,1:T(8,128)(2,1)}, bf16[4608,128]{1,0:T(8,128)(2,1)}) async-done(((bf16[1024,384]{1,0:T(8,128)(2,1)}, bf16[1024,128]{1,0:T(8,128)(2,1)}, bf16[1024,576]{0,1:T(8,128)(2,1)}, bf16[1024,576]{0,1:T(8,128)(2,1)}, bf16[4608,128]{1,0:T(8,128)(2,1)}), ...) | async-done | bytes 4587536 | tf_op jit(solution)/shard_map/psum | solution.py:204
  (218 shorter events, 123.7 us)
Async XLA Ops:
  7.2 11.9 copy-start.50
  7.2 30.0 %copy-start.51 = (bf16[128]{0:T(256)(128)(2,1)S(1)}, bf16[128]{0:T(256)(128)(2,1)}, u32[]{:S(2)}) copy-start(bf16[128]{0:T(256)(128)(2,1)} %param.20) | copy-start | bytes 772
  7.2 46.5 %copy-start.49 = (bf16[3,128]{1,0:T(4,128)(2,1)S(1)}, bf16[3,128]{1,0:T(4,128)(2,1)}, u32[]{:S(2)}) copy-start(bf16[3,128]{1,0:T(4,128)(2,1)} %param.18) | copy-start | bytes 2308
  7.2 64.9 %copy-start.4 = (bf16[2,256,1024]{2,1,0:T(8,128)(2,1)S(1)}, bf16[2,256,1024]{2,1,0:T(8,128)(2,1)}, u32[]{:S(2)}) copy-start(bf16[2,256,1024]{2,1,0:T(8,128)(2,1)} %param.11) | copy-start | bytes 3145732
  7.2 105.7 %all-gather.8.cloned.1.call-start = ((), (), s32[]{:S(2)}) async-start(), calls=%async_computation.6 | async-start | bytes 7077888 | tf_op jit(solution)/shard_map/all_gather | solution.py:181
  8.0 156.5 %all-gather.10.cloned.1.call-start = ((), (), s32[]{:S(2)}) async-start(), calls=%async_computation.7 | async-start | bytes 2359296 | tf_op jit(solution)/shard_map/all_gather | solution.py:182
  8.7 294.2 %all-gather.12.cloned.1.call-start = ((), (), s32[]{:S(2)}) async-start(), calls=%async_computation.8 | async-start | bytes 10616832 | tf_op jit(solution)/shard_map/all_gather | solution.py:183
  9.4 431.8 %all-gather.14.cloned.1.call-start = ((), (), s32[]{:S(2)}) async-start(), calls=%async_computation.9 | async-start | bytes 10616832 | tf_op jit(solution)/shard_map/all_gather | solution.py:184
  10.0 569.5 %all-gather.16.cloned.1.call-start = ((), (), s32[]{:S(2)}) async-start(), calls=%async_computation.10 | async-start | bytes 10616832 | tf_op jit(solution)/shard_map/all_gather | solution.py:185
  10.6 781.1 %reduce-scatter.21.cloned.1.call-start = ((), (), s32[]{:S(2)}) async-start(), calls=%async_computation.14 | async-start | bytes 2359296
  10.8 62.8 %collective-permute-start = (f32[2]{0:T(128)S(1)}, f32[2]{0:T(128)S(1)}, u32[]{:S(2)}, u32[]{:S(2)}) collective-permute-start(f32[2]{0:T(128)S(1)} %slice_bitcast_fusion.1), channel_id=1, source_target_pairs={{0,1},{1,2},{2,3},{3,4},{4,5},{5,6},{6,7},{8,9},{9,10},{10,11},{11... | collective-permute-start | bytes 32 | tf_op jit(solution)/shard_map/ppermute | solution.py:12
  15.7 58.0 %collective-permute-start.2 = (f32[2]{0:T(128)S(1)}, f32[2]{0:T(128)S(1)}, u32[]{:S(2)}, u32[]{:S(2)}) collective-permute-start(f32[2]{0:T(128)S(1)} %slice_bitcast_fusion), channel_id=1, source_target_pairs={{0,1},{1,2},{2,3},{3,4},{4,5},{5,6},{6,7},{8,9},{9,10},{10,11},{11... | collective-permute-start | bytes 32 | tf_op jit(solution)/shard_map/ppermute | solution.py:12
  118.0 7.6 collective-permute-start.1
  123.4 3.3 collective-permute-start.3
  128.9 39.8 %copy-start.31 = (bf16[256,1024]{1,0:T(8,128)(2,1)}, bf16[256,1024]{1,0:T(8,128)(2,1)S(1)}, u32[]{:S(2)}) copy-start(bf16[256,1024]{1,0:T(8,128)(2,1)S(1)} %get-tuple-element.40) | copy-start | bytes 1572868
  128.9 39.8 %copy-start.37 = (bf16[256,1024]{1,0:T(8,128)(2,1)}, bf16[256,1024]{1,0:T(8,128)(2,1)S(1)}, u32[]{:S(2)}) copy-start(bf16[256,1024]{1,0:T(8,128)(2,1)S(1)} %get-tuple-element.69) | copy-start | bytes 1572868
  167.0 135.9 %copy-start.15 = (f32[256,1024]{1,0:T(8,128)}, f32[256,1024]{1,0:T(8,128)S(1)}, u32[]{:S(2)}) copy-start(f32[256,1024]{1,0:T(8,128)S(1)} %get-tuple-element.90) | copy-start | bytes 3145732
  168.9 272.3 %copy-start.11 = (bf16[256,1024]{1,0:T(8,128)(2,1)}, bf16[256,1024]{1,0:T(8,128)(2,1)S(1)}, u32[]{:S(2)}) copy-start(bf16[256,1024]{1,0:T(8,128)(2,1)S(1)} %multiply_convert_fusion.14) | copy-start | bytes 1572868
  314.4 265.2 %copy-start.12 = (bf16[2,256,1024]{2,1,0:T(8,128)(2,1)S(1)}, bf16[2,256,1024]{2,1,0:T(8,128)(2,1)}, u32[]{:S(2)}) copy-start(bf16[2,256,1024]{2,1,0:T(8,128)(2,1)} %param.21) | copy-start | bytes 3145732
  656.6 186.7 %reduce-scatter.19.cloned.1.call-start = ((), (), s32[]{:S(2)}) async-start(), calls=%async_computation.13 | async-start | bytes 7077888
  662.3 11.2 copy-start.29
  664.4 11.1 copy-start.26
  664.9 5.5 collective-permute-start.4
  666.9 6.2 collective-permute-start.5
  688.6 320.9 %reduce-scatter.23.cloned.1.call-start = ((), (), s32[]{:S(2)}) async-start(), calls=%async_computation.15 | async-start | bytes 10616832
  688.8 10.9 copy-start.14
  723.9 451.8 %reduce-scatter.17.cloned.1.call-start = ((), (), s32[]{:S(2)}) async-start(), calls=%async_computation.12 | async-start | bytes 10616832 | tf_op jit(solution)/shard_map/reduce_scatter | solution.py:198
  748.9 592.9 %reduce-scatter.15.cloned.1.call-start = ((), (), s32[]{:S(2)}) async-start(), calls=%async_computation.11 | async-start | bytes 10616832 | tf_op jit(solution)/shard_map/reduce_scatter | solution.py:198
  774.2 631.3 %reduce-scatter.25.cloned.1.call-start = ((), (), s32[]{:S(2)}) async-start(), calls=%async_computation.16 | async-start | bytes 294912
  777.1 723.2 %all-reduce.15.cloned.1.call-start = ((), (), s32[]{:S(2)}) async-start(), calls=%async_computation.17 | async-start | bytes 9175040 | tf_op jit(solution)/shard_map/psum | solution.py:204
  1347.1 26.0 %copy-start.45 = (f32[256]{0:T(256)S(1)}, f32[256]{0:T(256)}, u32[]{:S(2)}) copy-start(f32[256]{0:T(256)} %get-tuple-element.81) | copy-start | bytes 3076
  1347.1 26.0 %copy-start.46 = (f32[256]{0:T(256)S(1)}, f32[256]{0:T(256)}, u32[]{:S(2)}) copy-start(f32[256]{0:T(256)} %get-tuple-element.83) | copy-start | bytes 3076
  (40 other events, 180.5 us)
Sparse Core Ops, SparseCore 0:
  10.1 102.7 all-gather.7
  115.0 49.4 all-gather.9
  166.6 136.2 all-gather.11
  304.9 136.2 all-gather.13
  443.1 136.3 all-gather.15
  656.7 65.9 reduce-scatter.20
  726.3 116.9 reduce-scatter.18
  846.9 162.5 reduce-scatter.22
  1013.1 162.5 reduce-scatter.16
  1179.2 162.5 reduce-scatter.14
  1345.1 60.3 reduce-scatter.24
  1408.6 91.6 all-reduce.14
